TPU v7x, 32 devices: a whole 2x2x4 slice. The times are simulated.
32 devices in a mesh: row: 8 (over y, x, core), cls: 4 (over z).
Axes of the slice: x: 2, y: 2, z: 4, core: 2. Of those that a mesh axis runs over, the one named last changes fastest.
Arguments:
- hidden: bfloat16 [10240, 2048], P(('row', 'cls')), as said below
- labels: int32 [10240, 4], P('row'), may hold values from 0 to 4095
- weights: bfloat16 [2048, 4096], P('row', 'cls'), may hold values from -0.125 to 0.125
- bias: float32 [4096], P('cls'), may hold values from -3 to 1
- direction: bfloat16 [2048, 4096], P('row', 'cls'), may hold values from -6 to 6
Outputs:
- gradient: float32 [2048, 4096], P('row', 'cls')
- precond: float32 [2048, 4096], P('row', 'cls')
- hvp: float32 [2048, 4096], P('row', 'cls')
Inputs may be any that keep to these rules, and one draw needn't show every extreme that they name: hidden states: entries independent up to an offset for each feature, with a positive scale for each context and for each feature.
All inputs are finite; a program needn't handle non-finite values.
Results may differ from a plain program's by a relative error of at most 0.0019.
Values may be sent and summed in bfloat16 or wider, within the bound.
A program may use at most 128 MiB of HBM per device.

v0:
```python
import jax
import jax.numpy as jnp
from jax import lax
from jax.sharding import PartitionSpec as P


def contract_rows(left, right):
    return lax.dot_general(
        left, right, (((0,), (0,)), ((), ())), preferred_element_type=jnp.float32
    )


def row_operands(block_h, block_y, whole_w, bias):
    logits = jnp.dot(block_h, whole_w, preferred_element_type=jnp.float32) + bias[None, :]
    probs = jax.nn.sigmoid(logits)
    residual = (probs - block_y).astype(jnp.bfloat16)
    curvature = probs * (1.0 - probs)
    curv_low = curvature.astype(jnp.bfloat16)
    squares = (block_h.astype(jnp.float32) * block_h.astype(jnp.float32)).astype(jnp.bfloat16)
    return (residual, curvature, curv_low, squares)


def first_pass(block_h, block_y, whole_w, bias):
    residual, curvature, curv_low, squares = row_operands(block_h, block_y, whole_w, bias)
    return (contract_rows(block_h, residual), contract_rows(squares, curv_low), curvature)


def second_pass(block_h, curvature, whole_v):
    projected = jnp.dot(block_h, whole_v, preferred_element_type=jnp.float32)
    weighted = (curvature * projected).astype(jnp.bfloat16)
    return contract_rows(block_h, weighted)


def body(hidden, labels, weights, bias, direction):
    whole_w, whole_v = (
        lax.all_gather(weights, "row", axis=0, tiled=True),
        lax.all_gather(direction, "row", axis=0, tiled=True),
    )
    cls_width = weights.shape[1]
    class_first = lax.axis_index("cls") * cls_width
    class_ids = class_first + lax.iota(jnp.int32, cls_width)
    targets = jnp.any(labels[:, :, None] == class_ids[None, None, :], axis=1).astype(jnp.float32)
    rows_h = lax.all_gather(hidden, "cls", axis=0, tiled=True)
    grad_sum, diag_sum, curvature = first_pass(rows_h, targets, whole_w, bias)
    hvp_sum = second_pass(rows_h, curvature, whole_v)
    grad_share, diag_share, hvp_share = (
        lax.psum_scatter(grad_sum, "row", scatter_dimension=0, tiled=True),
        lax.psum_scatter(diag_sum, "row", scatter_dimension=0, tiled=True),
        lax.psum_scatter(hvp_sum, "row", scatter_dimension=0, tiled=True),
    )
    row_count = jnp.float32(labels.shape[0] * lax.axis_size("row"))
    gradient = grad_share / jnp.sqrt(row_count)
    precond = gradient / (diag_share / row_count + 0.1)
    hvp = hvp_share / row_count
    return (gradient, precond, hvp)


def solution(mesh):
    return jax.shard_map(
        body,
        mesh=mesh,
        in_specs=(
            P(("row", "cls"), None),
            P("row", None),
            P("row", "cls"),
            P("cls"),
            P("row", "cls"),
        ),
        out_specs=(P("row", "cls"), P("row", "cls"), P("row", "cls")),
        check_vma=False,
    )
```

profile of v0, /device:TPU:0, one launch (start us, length us, event | category | flops | bytes accessed | tf_op | source)
XLA Modules:
  0.0 419.7 jit_solution(14975530918332369513)
XLA Ops:
  7.2 0.7 all-gather.6.cloned.1.call-update
  7.9 0.7 all-gather.4.cloned.1.call-update
  8.6 0.0 all-gather.8.cloned.1.call-start
  8.7 0.7 all-gather.8.cloned.1.call-update
  9.4 0.0 reduce-scatter.4.cloned.1.call-start
  9.4 4.5 %compare_reduce_fusion = pred[1280,1024]{1,0:T(8,128)(4,1)S(1)} fusion(s32[1024]{0:T(1024)S(1)} %iota_add_fusion, s32[1280,4]{0,1:T(4,128)} %param.6), kind=kLoop, calls=%fused_computation | loop fusion | flops 9175040 | bytes 1335296 | tf_op jit(solution)/shard_map/reduce_or | solution.py:42
  13.9 35.4 %all-gather.6.cloned.1.call-done = bf16[2048,1024]{1,0:T(8,128)(2,1)} async-done(((bf16[256,1024]{1,0:T(8,128)(2,1)}), bf16[2048,1024]{1,0:T(8,128)(2,1)}) %all-gather.6.cloned.1.call-update) | async-done | bytes 4194320 | tf_op jit(solution)/shard_map/all_gather | solution.py:36
  49.3 99.7 %all-gather.4.cloned.1.call-done = bf16[1280,2048]{1,0:T(8,128)(2,1)} async-done(((bf16[320,2048]{1,0:T(8,128)(2,1)}), bf16[1280,2048]{1,0:T(8,128)(2,1)}) %all-gather.4.cloned.1.call-update) | async-done | bytes 5242896 | tf_op jit(solution)/shard_map/all_gather | solution.py:43
  149.0 9.5 %add_divide_fusion = f32[1280,1024]{1,0:T(8,128)S(1)} fusion(bf16[1280,2048]{1,0:T(8,128)(2,1)} %all-gather.4.cloned.1.call-done, bf16[2048,1024]{1,0:T(8,128)(2,1)} %all-gather.6.cloned.1.call-done, f32[1024]{0:T(1024)} %param.8), kind=kOutput, calls=%fused_computation.6 | convolution fusion | flops 5373952000 | bytes 14684160 | tf_op jit(solution)/shard_map/dot_general | solution.py:14
  158.5 2.3 copy-done.1
  160.8 8.2 %convolution_bitcast_fusion.1 = f32[2048,1024]{0,1:T(8,128)} fusion(bf16[1280,2048]{1,0:T(8,128)(2,1)S(1)} %copy-done, f32[1280,1024]{1,0:T(8,128)S(1)} %add_divide_fusion, pred[1280,1024]{1,0:T(8,128)(4,1)S(1)} %compare_reduce_fusion), kind=kOutput, calls=%fused_computation.9 | convolution fusion | flops 5372641280 | bytes 20185088 | tf_op jit(solution)/shard_map/dot_general | solution.py:8
  169.0 0.0 reduce-scatter.6.cloned.1.call-start
  169.1 11.9 %fusion = f32[2048,1024]{0,1:T(8,128)} fusion(bf16[1280,2048]{1,0:T(8,128)(2,1)} %all-gather.4.cloned.1.call-done, f32[1280,1024]{1,0:T(8,128)} %copy-done.1), kind=kOutput, calls=%fused_computation.3 | convolution fusion | flops 5380505600 | bytes 18874368 | tf_op jit(solution)/shard_map/dot_general | solution.py:8
  181.0 0.2 reduce-scatter.8.cloned.1.call-start
  181.3 4.8 %all-gather.8.cloned.1.call-done = bf16[2048,1024]{1,0:T(8,128)(2,1)} async-done(((bf16[256,1024]{1,0:T(8,128)(2,1)}), bf16[2048,1024]{1,0:T(8,128)(2,1)}) %all-gather.8.cloned.1.call-update) | async-done | bytes 4194320 | tf_op jit(solution)/shard_map/all_gather | solution.py:37
  186.0 20.0 %convolution_bitcast_fusion = f32[2048,1024]{0,1:T(8,128)} fusion(bf16[1280,2048]{1,0:T(8,128)(2,1)} %all-gather.4.cloned.1.call-done, bf16[2048,1024]{1,0:T(8,128)(2,1)} %all-gather.8.cloned.1.call-done, f32[1280,1024]{1,0:T(8,128)} %copy-done.1), kind=kOutput, calls=%fused_computation.8 | convolution fusion | flops 10742661120 | bytes 23068672 | tf_op jit(solution)/shard_map/dot_general | solution.py:8
  206.1 54.6 %reduce-scatter.4.cloned.1.call-done = f32[256,1024]{0,1:T(8,128)} async-done(((f32[2048,1024]{0,1:T(8,128)}), f32[256,1024]{0,1:T(8,128)}) %reduce-scatter.4.cloned.1.call-update) | async-done | bytes 1048592 | tf_op jit(solution)/shard_map/reduce_scatter | solution.py:47
  260.6 75.0 %reduce-scatter.6.cloned.1.call-done = f32[256,1024]{0,1:T(8,128)} async-done(((f32[2048,1024]{0,1:T(8,128)}), f32[256,1024]{0,1:T(8,128)}) %reduce-scatter.6.cloned.1.call-update) | async-done | bytes 1048592 | tf_op jit(solution)/shard_map/reduce_scatter | solution.py:48
  335.6 1.8 add_divide_fusion.1
  337.4 1.3 copy.14
  338.7 1.3 copy.15
  340.0 70.2 %reduce-scatter.8.cloned.1.call-done = f32[256,1024]{0,1:T(8,128)} async-done(((f32[2048,1024]{0,1:T(8,128)}), f32[256,1024]{0,1:T(8,128)}) %reduce-scatter.8.cloned.1.call-update) | async-done | bytes 1048592 | tf_op jit(solution)/shard_map/reduce_scatter | solution.py:49
  410.2 1.3 broadcast_multiply_fusion
  411.6 1.3 copy.16
  (9 shorter events, 0.1 us)
Async XLA Ops:
  7.2 42.2 %all-gather.6.cloned.1.call-start = ((), (), s32[]{:S(2)}) async-start(), calls=%async_computation.4 | async-start | bytes 4718592 | tf_op jit(solution)/shard_map/all_gather | solution.py:36
  7.9 141.1 %all-gather.4.cloned.1.call-start = ((), (), s32[]{:S(2)}) async-start(), calls=%async_computation.3 | async-start | bytes 6553600 | tf_op jit(solution)/shard_map/all_gather | solution.py:43
  8.6 177.4 %all-gather.8.cloned.1.call-start = ((), (), s32[]{:S(2)}) async-start(), calls=%async_computation.7 | async-start | bytes 4718592 | tf_op jit(solution)/shard_map/all_gather | solution.py:37
  9.4 251.3 %reduce-scatter.4.cloned.1.call-start = ((), (), s32[]{:S(2)}) async-start(), calls=%async_computation.5 | async-start | bytes 9437184 | tf_op jit(solution)/shard_map/reduce_scatter | solution.py:47
  149.0 11.8 %copy-start = (bf16[1280,2048]{1,0:T(8,128)(2,1)S(1)}, bf16[1280,2048]{1,0:T(8,128)(2,1)}, u32[]{:S(2)}) copy-start(bf16[1280,2048]{1,0:T(8,128)(2,1)} %all-gather.4.cloned.1.call-done) | copy-start | bytes 15728644
  158.5 2.3 copy-start.1
  169.0 166.6 %reduce-scatter.6.cloned.1.call-start = ((), (), s32[]{:S(2)}) async-start(), calls=%async_computation.6 | async-start | bytes 9437184 | tf_op jit(solution)/shard_map/reduce_scatter | solution.py:48
  181.0 229.2 %reduce-scatter.8.cloned.1.call-start = ((), (), s32[]{:S(2)}) async-start(), calls=%async_computation.8 | async-start | bytes 9437184 | tf_op jit(solution)/shard_map/reduce_scatter | solution.py:49
Sparse Core Ops, SparseCore 0:
  9.9 39.4 all-gather.5
  50.9 98.0 all-gather.3
  150.9 35.0 all-gather.7
  189.3 71.2 reduce-scatter.3
  264.3 71.2 reduce-scatter.5
  339.0 71.2 reduce-scatter.7
where the time goes:
time: 420 us
  waiting for transfers between devices  342 us (81%)
  matrix products  49.7 us (12%)
  between operations  14.2 us (3%)
  other arithmetic  7.58 us (2%)
  local copies, waits for them, and re-layouts  6.2 us (1%)
    all_gather x1, waiting for transfers between devices, body(): rows_h = lax.all_gather(hidden, 'cls', axis=0, tiled=True)  99.7 us
    reduce_scatter x1, waiting for transfers between devices, body(): lax.psum_scatter(diag_sum, 'row', scatter_dimension=0, tiled=True)  75 us
    reduce_scatter x1, waiting for transfers between devices, body(): lax.psum_scatter(hvp_sum, 'row', scatter_dimension=0, tiled=True)  70.2 us
    reduce_scatter x1, waiting for transfers between devices, body(): lax.psum_scatter(grad_sum, 'row', scatter_dimension=0, tiled=True)  54.6 us
    dot_general x3, matrix products, contract_rows(): lax.dot_general(left, right, (((0,), (0,)), ((), ())), preferred_element_...  40.2 us
    all_gather x1, waiting for transfers between devices, body(): lax.all_gather(weights, 'row', axis=0, tiled=True)  35.4 us
    dot_general x1, matrix products, row_operands(): jnp.dot(block_h, whole_w, preferred_element_type=jnp.float32)  9.46 us
  transfers between devices with their start and end apart: 6, of which 6 were waited for; matrix products, arithmetic and copies ran while one was open for 14% of the time, Pallas kernels for 0%

commit v1 on v0

v1 whole, which is shorter than its diff:
```python
import functools
import math

import jax
import jax.numpy as jnp
from jax import lax
from jax.experimental import pallas as pl
from jax.experimental.pallas import tpu as pltpu
from jax.sharding import PartitionSpec as P

MESH = pl.DeviceIdType.MESH
F32 = jnp.float32
BF16 = jnp.bfloat16


def bits_of(mask):
    return [1 << i for i in range(mask.bit_length()) if (mask >> i) & 1]


def flip(r, mask):
    for b in bits_of(mask):
        r = r + b - 2 * b * lax.rem(lax.div(r, b), 2)
    return r


def first_of(mask, order):
    for i, b in enumerate(order):
        if mask & b:
            return i
    return len(order)


def kernel(R, Z, Q, lab, bias, hid, wts, dirn, g_out, p_out, v_out,
           H, WV, RHS, LT, TMP, CS, CR, SS, SR,
           loc_sem, w_send, w_recv, up_send, dn_send, h_recv,
           c_send, c_recv, s_send, s_recv):
    r = lax.axis_index("row")
    z = lax.axis_index("cls")
    T = hid.shape[0]
    D = hid.shape[1]
    F, C = wts.shape
    CH = C // 2
    TQ = T // Q
    ici = [1 << i for i in range(1, R.bit_length() - 1)]
    orders = (ici, ici[::-1])
    n = len(ici)
    masks = [2 * i for i in range(R // 2)]
    up, dn = lax.rem(z + 1, Z), lax.rem(z + Z - 1, Z)
    has_up, has_dn = z < Z - 1, z > 0

    def hrows(k, q):
        return pl.ds(pl.multiple_of(k * T + q * TQ, TQ), TQ)

    def frows(s):
        return pl.ds(pl.multiple_of(s * F, F), F)

    srcs = (wts, dirn)
    locals_ = [pltpu.make_async_copy(hid, H.at[pl.ds(pl.multiple_of(z * T, T), T), :], loc_sem.at[0])]
    for a in range(2):
        locals_.append(pltpu.make_async_copy(srcs[a], WV.at[a, frows(r), :], loc_sem.at[1 + a]))
    for c in locals_:
        c.start()

    barrier = pltpu.get_barrier_semaphore()
    for b in [1] + ici:
        pl.semaphore_signal(barrier, inc=1, device_id=(flip(r, b), z), device_id_type=MESH)

    @pl.when(has_up)
    def _():
        pl.semaphore_signal(barrier, inc=1, device_id=(r, up), device_id_type=MESH)

    @pl.when(has_dn)
    def _():
        pl.semaphore_signal(barrier, inc=1, device_id=(r, dn), device_id_type=MESH)

    pl.semaphore_wait(barrier, n + 1 + jnp.where(has_up, 1, 0) + jnp.where(has_dn, 1, 0))

    def h_copy(k, q, upward, own=False):
        rows = hrows(k, q)
        return pltpu.make_async_remote_copy(
            src_ref=hid.at[pl.ds(q * TQ, TQ), :] if own else H.at[rows, :],
            dst_ref=H.at[rows, :],
            send_sem=(up_send if upward else dn_send).at[k, q],
            recv_sem=h_recv.at[k, q],
            device_id=(r, up if upward else dn),
            device_id_type=MESH,
        )

    def h_own(q):
        @pl.when(has_up)
        def _():
            h_copy(z, q, True, own=True).start()

        @pl.when(has_dn)
        def _():
            h_copy(z, q, False, own=True).start()

    def h_pass(k, q, from_below):
        h_copy(k, q, from_below).wait_recv()

        @pl.when(has_up if from_below else has_dn)
        def _():
            h_copy(k, q, from_below).start()

    w_orders = (ici + [1], ici[::-1] + [1])
    w_started = []

    def w_copy(a, mask, to):
        rows = frows(flip(r, mask))
        return pltpu.make_async_remote_copy(
            src_ref=WV.at[a, rows, :] if mask else srcs[a],
            dst_ref=WV.at[a, rows, :],
            send_sem=w_send.at[a, (mask | to) - 1],
            recv_sem=w_recv.at[a, (mask | to) - 1],
            device_id=(flip(r, to), z),
            device_id_type=MESH,
        )

    def w_forward(a, mask):
        order = w_orders[a]
        after = max([order.index(b) for b in bits_of(mask)], default=-1)
        for b in order[after + 1:]:
            c = w_copy(a, mask, b)
            c.start()
            w_started.append(c)

    def w_wait(a, mask):
        rows = frows(flip(r, mask))
        pltpu.make_async_remote_copy(
            src_ref=WV.at[a, rows, :], dst_ref=WV.at[a, rows, :],
            send_sem=w_send.at[a, mask - 1], recv_sem=w_recv.at[a, mask - 1],
            device_id=(flip(r, 1), z), device_id_type=MESH,
        ).wait_recv()

    for a in range(2):
        w_forward(a, 0)
    for q in range(Q):
        h_own(q)

    def h_pass_one(q):
        @pl.when(has_dn)
        def _():
            h_pass(z - 1, q, True)

        @pl.when(has_up)
        def _():
            h_pass(z + 1, q, False)

    arrivals = sorted([m for m in masks if m], key=lambda m: (len(bits_of(m)), m))
    for pos, m in enumerate(arrivals):
        for a in range(2):
            mm = m if a == 0 else sum(ici[n - 1 - ici.index(b)] for b in bits_of(m))
            w_wait(a, mm)
            w_forward(a, mm)
        if pos >= len(arrivals) - Q:
            h_pass_one(pos - (len(arrivals) - Q))
    for c in locals_:
        c.wait()
    for a in range(2):
        for m in masks:
            w_wait(a, m | 1)

    CB = min(256, C)
    class0 = z * C

    def operands(k):
        rows = pl.ds(pl.multiple_of(k * T, T), T)
        labels = lab[rows, :]
        for j in range(C // CB):
            cols = pl.ds(j * CB, CB)
            x = H[rows, :]
            logits = jnp.dot(x, WV[0, :, cols], preferred_element_type=F32) + bias[:, cols]
            ids = class0 + j * CB + lax.broadcasted_iota(jnp.int32, (T, CB), 1)
            hit = labels[:, 0:1] == ids
            for i in range(1, labels.shape[1]):
                hit = hit | (labels[:, i:i + 1] == ids)
            probs = jax.nn.sigmoid(logits)
            curv = probs * (1.0 - probs)
            RHS[0, rows, cols] = (probs - jnp.where(hit, 1.0, 0.0)).astype(BF16)
            RHS[1, rows, cols] = curv.astype(BF16)
            proj = jnp.dot(x, WV[1, :, cols], preferred_element_type=F32)
            RHS[2, rows, cols] = (curv * proj).astype(BF16)

    def step(t, carry):
        d = lax.div(t + 1, 2)
        below = lax.rem(t, 2) == 1
        k = jnp.where(below, z - d, z + d)

        @pl.when(jnp.logical_and(k >= 0, k < Z))
        def _():
            @pl.when(jnp.logical_and(d > 1, below))
            def _():
                for q in range(Q):
                    h_pass(k, q, True)

            @pl.when(jnp.logical_and(d > 1, jnp.logical_not(below)))
            def _():
                for q in range(Q):
                    h_pass(k, q, False)

            operands(k)
        return carry

    lax.fori_loop(0, 2 * Z - 1, step, 0)

    FB = max(F, 128)

    def left(s):
        base = lax.div(s * F, FB) * FB
        h = H[:, pl.ds(pl.multiple_of(base, FB), FB)].T
        LT[0] = h
        h32 = h.astype(F32)
        LT[1] = (h32 * h32).astype(BF16)
        return s * F - base

    def partial(off, a, h):
        p = jnp.dot(LT[a % 2], RHS[a, :, pl.ds(h * CH, CH)], preferred_element_type=F32)
        if FB == F:
            return p
        TMP[...] = p
        return TMP[pl.ds(pl.multiple_of(off, F), F), :]

    started = []

    turn = sorted(masks, key=lambda m: (-len(bits_of(m)), m))
    core_copies = {}

    def c_copy(m, a):
        return pltpu.make_async_remote_copy(
            src_ref=CS.at[turn.index(m) % 2, a], dst_ref=CR.at[m // 2, a],
            send_sem=c_send.at[m // 2, a], recv_sem=c_recv.at[m // 2, a],
            device_id=(flip(r, 1), z), device_id_type=MESH,
        )

    def s_copy(h, m, a, to):
        i = m // 2 - 1
        return pltpu.make_async_remote_copy(
            src_ref=SS.at[h, i, a], dst_ref=SR.at[h, i, a],
            send_sem=s_send.at[h, i, a], recv_sem=s_recv.at[h, i, a],
            device_id=(flip(r, to), z), device_id_type=MESH,
        )

    def other(m):
        off = left(flip(r, m | 1))
        for a in range(3):
            at = turn.index(m)
            if at >= 2:
                core_copies.pop((turn[at - 2], a)).wait_send()
            for h in range(2):
                CS[at % 2, a, :, pl.ds(h * CH, CH)] = partial(off, a, h)
            core_copies[m, a] = c_copy(m, a)
            core_copies[m, a].start()

    def send_stage(h, m, a, value):
        SS[h, m // 2 - 1, a] = value.astype(BF16)
        c = s_copy(h, m, a, orders[h][first_of(m, orders[h])])
        c.start()
        started.append(c)

    def mine(m):
        off = left(flip(r, m))
        for a in range(3):
            c_copy(m, a).wait_recv()
            for h in range(2):
                t = partial(off, a, h) + CR[m // 2, a, :, pl.ds(h * CH, CH)]
                if first_of(m, orders[h]) == 0 and n:
                    send_stage(h, m, a, t)
                else:
                    CR[m // 2, a, :, pl.ds(h * CH, CH)] = t

    def gathered(h, m, a, upto):
        t = CR[m // 2, a, :, pl.ds(h * CH, CH)]
        for j in range(upto):
            src = m | orders[h][j]
            s_copy(h, src, a, orders[h][j]).wait_recv()
            t = t + SR[h, src // 2 - 1, a].astype(F32)
        return t

    other(turn[0])
    for i, m in enumerate(turn):
        if i + 1 < len(turn):
            other(turn[i + 1])
        mine(m)
    for i in range(1, n):
        for m in turn:
            for a in range(3):
                for h in range(2):
                    if m and first_of(m, orders[h]) == i:
                        send_stage(h, m, a, gathered(h, m, a, i))

    count = float(T * Z * R)
    for h in range(2):
        cols = pl.ds(h * CH, CH)
        grad = gathered(h, 0, 0, n) * (1.0 / math.sqrt(count))
        g_out[:, cols] = grad
        p_out[:, cols] = grad / (gathered(h, 0, 1, n) * (1.0 / count) + 0.1)
        v_out[:, cols] = gathered(h, 0, 2, n) * (1.0 / count)

    for c in w_started + started + list(core_copies.values()):
        c.wait_send()

    def drain(k, carry):
        for q in range(Q):
            @pl.when(jnp.logical_and(has_up, k <= z))
            def _():
                h_copy(k, q, True).wait_send()

            @pl.when(jnp.logical_and(has_dn, k >= z))
            def _():
                h_copy(k, q, False).wait_send()
        return carry

    lax.fori_loop(0, Z, drain, 0)


def body(R, Z, hidden, labels, weights, bias, direction):
    T, D = hidden.shape
    F, C = weights.shape
    Q = 2
    rows = T * Z
    FB = max(F, 128)
    n_masks = R // 2
    out = jax.ShapeDtypeStruct((F, C), F32)
    vmem = pl.BlockSpec(memory_space=pltpu.VMEM)
    hbm = pl.BlockSpec(memory_space=pl.ANY)
    dma = pltpu.SemaphoreType.DMA
    return pl.pallas_call(
        functools.partial(kernel, R, Z, Q),
        out_shape=(out, out, out),
        in_specs=[vmem, vmem, hbm, hbm, hbm],
        out_specs=(vmem, vmem, vmem),
        scratch_shapes=[
            pltpu.VMEM((rows, D), BF16),
            pltpu.VMEM((2, F * R, C), BF16),
            pltpu.VMEM((3, rows, C), BF16),
            pltpu.VMEM((2, FB, rows), BF16),
            pltpu.VMEM((FB, C // 2) if FB != F else (8, 128), F32),
            pltpu.VMEM((2, 3, F, C), F32),
            pltpu.VMEM((n_masks, 3, F, C), F32),
            pltpu.VMEM((2, n_masks - 1, 3, F, C // 2), BF16),
            pltpu.VMEM((2, n_masks - 1, 3, F, C // 2), BF16),
            dma((3,)),
            dma((2, R - 1)),
            dma((2, R - 1)),
            dma((Z, Q)),
            dma((Z, Q)),
            dma((Z, Q)),
            dma((n_masks, 3)),
            dma((n_masks, 3)),
            dma((2, n_masks - 1, 3)),
            dma((2, n_masks - 1, 3)),
        ],
        compiler_params=pltpu.CompilerParams(
            collective_id=0, has_side_effects=True, vmem_limit_bytes=62 * 1024 * 1024
        ),
        cost_estimate=pl.CostEstimate(
            flops=10 * rows * D * C, bytes_accessed=2 * T * D + 4 * F * C + 12 * F * C,
            transcendentals=rows * C,
        ),
    )(labels, bias.reshape(1, C), hidden, weights, direction)


def solution(mesh):
    return jax.shard_map(
        functools.partial(body, mesh.shape["row"], mesh.shape["cls"]),
        mesh=mesh,
        in_specs=(
            P(("row", "cls"), None),
            P("row", None),
            P("row", "cls"),
            P("cls"),
            P("row", "cls"),
        ),
        out_specs=(P("row", "cls"), P("row", "cls"), P("row", "cls")),
        check_vma=False,
    )
```

time: 420 us -> 163 us (0.39)
  waiting for transfers between devices: 342 us -> 0 us
  Pallas kernels: 0 us -> 156 us
  matrix products: 49.7 us -> 0 us
  between operations: 14.2 us -> 0.65 us
  other arithmetic: 7.58 us -> 0 us
    reduce_scatter x3 -> x0, waiting for transfers between devices: 200 us -> none  [the longest x1 75 us: body(): lax.psum_scatter(diag_sum, 'row', scatter_dimension=0, tiled=True)]
    pallas_call x0 -> x1, Pallas kernels: none -> 156 us  [body(): pl.pallas_call(functools.partial(kernel, R, Z, Q), out_shape=(out, out, o...]
    all_gather x3 -> x0, waiting for transfers between devices: 140 us -> none  [the longest x1 99.7 us: body(): rows_h = lax.all_gather(hidden, 'cls', axis=0, tiled=True)]
    dot_general x4 -> x0, matrix products: 49.7 us -> none  [the longest x3 40.2 us: contract_rows(): lax.dot_general(left, right, (((0,), (0,)), ((), ())), preferred_element_...]
    reduce_or x1 -> x0, other arithmetic: 4.49 us -> none  [body(): jnp.any(labels[:, :, None] == class_ids[None, None, :], axis=1)]
  transfers between devices with their start and end apart: 6 -> 0, of which waited for: 6 -> 0; matrix products, arithmetic and copies ran while one was open for 14% -> 0% of each run, Pallas kernels for 0% -> 0%
where the time goes in v1:
time: 163 us
  Pallas kernels  156 us (96%)
  local copies, waits for them, and re-layouts  6.8 us (4%)
    pallas_call x1, Pallas kernels, body(): pl.pallas_call(functools.partial(kernel, R, Z, Q), out_shape=(out, out, o...  156 us
    unnamed x8, local copies, waits for them, and re-layouts  6.8 us

profile of v1, /device:TPU:0, one launch (start us, length us, event | category | flops | bytes accessed | tf_op | source)
XLA Modules:
  0.0 163.2 jit_solution(453165031417911700)
XLA Ops:
  0.6 1.8 %copy.8.lab = s32[1280,4]{1,0:T(8,128)} copy(s32[1280,4]{0,1:T(4,128)} %param.6) | data formatting | bytes 40960 | tf_op args[1]
  2.5 155.7 %shard_map.76 = (f32[256,1024]{1,0:T(8,128)}, f32[256,1024]{1,0:T(8,128)}, f32[256,1024]{1,0:T(8,128)}) custom-call(s32[1280,4]{1,0:T(8,128)} %copy.8.lab, f32[1,1024]{1,0:T(1,128)} %bitcast.1, bf16[320,2048]{1,0:T(8,128)(2,1)} %hid.1, bf16[256,1024]{1,0:T(8,128)(2,1)} %wts.1, bf16[256,1024]{1,0:T(8,128)(2,1)} %dirn.1), custom_call_target="tpu_custom_call" | custom-call | flops 26843545600 | bytes 5505024 | tf_op jit(solution)/shard_map/pallas_call | solution.py:327
  158.2 0.0 copy-start.1
  158.2 2.4 %copy.12 = f32[256,1024]{1,0:T(8,128)} copy(f32[256,1024]{1,0:T(8,128)} %get-tuple-element.6) | data formatting | bytes 2097152
  160.6 0.0 copy-done.1
  160.6 0.0 copy-start
  160.6 1.0 copy.13
  161.6 0.6 copy-done
  162.2 1.0 copy.14
Async XLA Ops:
  158.2 2.4 %copy-start.1 = (f32[256,1024]{1,0:T(8,128)S(1)}, f32[256,1024]{1,0:T(8,128)}, u32[]{:S(2)}) copy-start(f32[256,1024]{1,0:T(8,128)} %get-tuple-element.7) | copy-start | bytes 3145732
  160.6 1.6 copy-start

commit v2 on v1

--- a/solution.py
+++ b/solution.py
@@ -30,8 +30,8 @@
     return len(order)
 
 
-def kernel(R, Z, Q, lab, bias, hid, wts, dirn, g_out, p_out, v_out,
-           H, WV, RHS, LT, TMP, CS, CR, SS, SR,
+def kernel(R, Z, Q, lab, bias, hid, wts, dirn, sums_out,
+           H, WV, RHS, LT, TMP, CS, CR, SS, SR, LAB,
            loc_sem, w_send, w_recv, up_send, dn_send, h_recv,
            c_send, c_recv, s_send, s_recv):
     r = lax.axis_index("row")
@@ -136,6 +136,7 @@
         w_forward(a, 0)
     for q in range(Q):
         h_own(q)
+    LAB[...] = lab[...].T
 
     def h_pass_one(q):
         @pl.when(has_dn)
@@ -147,13 +148,17 @@
             h_pass(z + 1, q, False)
 
     arrivals = sorted([m for m in masks if m], key=lambda m: (len(bits_of(m)), m))
-    for pos, m in enumerate(arrivals):
-        for a in range(2):
-            mm = m if a == 0 else sum(ici[n - 1 - ici.index(b)] for b in bits_of(m))
-            w_wait(a, mm)
-            w_forward(a, mm)
-        if pos >= len(arrivals) - Q:
-            h_pass_one(pos - (len(arrivals) - Q))
+    def w_pass(some):
+        for m in some:
+            for a in range(2):
+                mm = m if a == 0 else sum(ici[n - 1 - ici.index(b)] for b in bits_of(m))
+                w_wait(a, mm)
+                w_forward(a, mm)
+
+    w_pass(arrivals[:n])
+    for q in range(Q):
+        h_pass_one(q)
+    w_pass(arrivals[n:])
     for c in locals_:
         c.wait()
     for a in range(2):
@@ -165,7 +170,7 @@
 
     def operands(k):
         rows = pl.ds(pl.multiple_of(k * T, T), T)
-        labels = lab[rows, :]
+        labels = LAB[rows, :]
         for j in range(C // CB):
             cols = pl.ds(j * CB, CB)
             x = H[rows, :]
@@ -276,11 +281,14 @@
             t = t + SR[h, src // 2 - 1, a].astype(F32)
         return t
 
-    other(turn[0])
-    for i, m in enumerate(turn):
-        if i + 1 < len(turn):
-            other(turn[i + 1])
+    ahead = turn[:-1]
+    other(ahead[0])
+    for i, m in enumerate(ahead):
+        if i + 1 < len(ahead):
+            other(ahead[i + 1])
         mine(m)
+    other(turn[-1])
+    mine(turn[-1])
     for i in range(1, n):
         for m in turn:
             for a in range(3):
@@ -288,13 +296,9 @@
                     if m and first_of(m, orders[h]) == i:
                         send_stage(h, m, a, gathered(h, m, a, i))
 
-    count = float(T * Z * R)
-    for h in range(2):
-        cols = pl.ds(h * CH, CH)
-        grad = gathered(h, 0, 0, n) * (1.0 / math.sqrt(count))
-        g_out[:, cols] = grad
-        p_out[:, cols] = grad / (gathered(h, 0, 1, n) * (1.0 / count) + 0.1)
-        v_out[:, cols] = gathered(h, 0, 2, n) * (1.0 / count)
+    for a in range(3):
+        for h in range(2):
+            sums_out[a, :, pl.ds(h * CH, CH)] = gathered(h, 0, a, n)
 
     for c in w_started + started + list(core_copies.values()):
         c.wait_send()
@@ -320,15 +324,14 @@
     rows = T * Z
     FB = max(F, 128)
     n_masks = R // 2
-    out = jax.ShapeDtypeStruct((F, C), F32)
     vmem = pl.BlockSpec(memory_space=pltpu.VMEM)
     hbm = pl.BlockSpec(memory_space=pl.ANY)
     dma = pltpu.SemaphoreType.DMA
-    return pl.pallas_call(
+    sums = pl.pallas_call(
         functools.partial(kernel, R, Z, Q),
-        out_shape=(out, out, out),
+        out_shape=jax.ShapeDtypeStruct((3, F, C), F32),
         in_specs=[vmem, vmem, hbm, hbm, hbm],
-        out_specs=(vmem, vmem, vmem),
+        out_specs=vmem,
         scratch_shapes=[
             pltpu.VMEM((rows, D), BF16),
             pltpu.VMEM((2, F * R, C), BF16),
@@ -339,6 +342,7 @@
             pltpu.VMEM((n_masks, 3, F, C), F32),
             pltpu.VMEM((2, n_masks - 1, 3, F, C // 2), BF16),
             pltpu.VMEM((2, n_masks - 1, 3, F, C // 2), BF16),
+            pltpu.VMEM((rows, labels.shape[1]), jnp.int32),
             dma((3,)),
             dma((2, R - 1)),
             dma((2, R - 1)),
@@ -357,7 +361,11 @@
             flops=10 * rows * D * C, bytes_accessed=2 * T * D + 4 * F * C + 12 * F * C,
             transcendentals=rows * C,
         ),
-    )(labels, bias.reshape(1, C), hidden, weights, direction)
+    )(labels.T, bias.reshape(1, C), hidden, weights, direction)
+    count = float(rows * R)
+    gradient = sums[0] * (1.0 / math.sqrt(count))
+    precond = gradient / (sums[1] * (1.0 / count) + 0.1)
+    return gradient, precond, sums[2] * (1.0 / count)
 
 
 def solution(mesh):

time: 163 us -> 161 us (0.988)
  local copies, waits for them, and re-layouts: 6.8 us -> 0 us
  other arithmetic: 0 us -> 5.63 us
    unnamed x8 -> x0, local copies, waits for them, and re-layouts: 6.8 us -> none
    div x0 -> x1, other arithmetic: none -> 3.28 us  [body(): precond = gradient / (sums[1] * (1.0 / count) + 0.1)]
    mul x0 -> x1, other arithmetic: none -> 2.34 us  [body(): return (gradient, precond, sums[2] * (1.0 / count))]
where the time goes in v2:
time: 161 us
  Pallas kernels  155 us (96%)
  other arithmetic  5.63 us (3%)
    pallas_call x1, Pallas kernels, body(): pl.pallas_call(functools.partial(kernel, R, Z, Q), out_shape=jax.ShapeDty...  155 us
    div x1, other arithmetic, body(): precond = gradient / (sums[1] * (1.0 / count) + 0.1)  3.28 us

profile of v2, /device:TPU:0, one launch (start us, length us, event | category | flops | bytes accessed | tf_op | source)
XLA Modules:
  0.0 161.2 jit_solution(1931680676116682730)
XLA Ops:
  0.6 154.9 %shard_map.76 = f32[3,256,1024]{2,1,0:T(8,128)} custom-call(s32[4,1280]{1,0:T(4,128)} %bitcast.9, f32[1,1024]{1,0:T(1,128)} %bitcast.10, bf16[320,2048]{1,0:T(8,128)(2,1)} %hid.1, bf16[256,1024]{1,0:T(8,128)(2,1)} %wts.1, bf16[256,1024]{1,0:T(8,128)(2,1)} %dirn.1), custom_call_target="tpu_custom_call" | custom-call | flops 26843545600 | bytes 5505024 | tf_op jit(solution)/shard_map/pallas_call | solution.py:330
  155.6 3.3 %bitcast_divide_fusion = (f32[256,1024]{1,0:T(8,128)}, f32[256,1024]{1,0:T(8,128)}) fusion(f32[3,256,1024]{2,1,0:T(8,128)} %shard_map.76), kind=kLoop, calls=%fused_computation | loop fusion | flops 1048576 | bytes 4194304 | tf_op jit(solution)/shard_map/div | solution.py:367
  158.9 2.3 %multiply_bitcast_fusion = f32[256,1024]{1,0:T(8,128)} fusion(f32[3,256,1024]{2,1,0:T(8,128)} %shard_map.76), kind=kLoop, calls=%fused_computation.1 | loop fusion | flops 262144 | bytes 2097152 | tf_op jit(solution)/shard_map/mul | solution.py:368
